TPU v7x, 256 devices: a whole 4x4x8 slice. The times are simulated.
256 devices in a mesh: patch: 64 (over x, z, core), feat: 4 (over y).
Axes of the slice: x: 4, y: 4, z: 8, core: 2. Of those that a mesh axis runs over, the one named last changes fastest.
Arguments:
- nodes: bfloat16 [40960, 512], P(('patch', 'feat')), may hold values from -6 to 6
- edges: bfloat16 [327680, 512], P(('patch', 'feat')), may hold values from -6 to 6
- receivers: int32 [327680], P(('patch', 'feat')), may hold values from 0 to 639
- sender_slot: int32 [327680], P(('patch', 'feat')), may hold values from 0 to 2175
- send_rows: int32 [64, 4, 64, 24], P('patch', 'feat'), may hold values from 0 to 159
- live_edges: int32 [256], P(('patch', 'feat')), may hold values from 1 to 1280, 245760 in all
- edge_w1: bfloat16 [1536, 512], replicated, may hold values from -0.15625 to 0.15625
- edge_b1: float32 [512], replicated, may hold values from -3 to 3
- edge_w2: bfloat16 [512, 512], replicated, may hold values from -0.25 to 0.25
- edge_gain: float32 [512], replicated, may hold values from 0.5 to 1.5
- node_w1: bfloat16 [1024, 512], replicated, may hold values from -0.1875 to 0.1875
- node_b1: float32 [512], replicated, may hold values from -3 to 3
- node_w2: bfloat16 [512, 512], replicated, may hold values from -0.25 to 0.25
- node_gain: float32 [512], replicated, may hold values from 0.5 to 1.5
Outputs:
- edges_out: bfloat16 [327680, 512], P(('patch', 'feat'))
- nodes_out: bfloat16 [40960, 512], P(('patch', 'feat'))
Inputs may be any that keep to these rules, and one draw needn't show every extreme that they name: `live_edges`: edge slots at or past a device's count are padding.
All inputs are finite; a program needn't handle non-finite values.
Results may differ from a plain program's by a relative error of at most 0.0052.
Values may be sent and summed in bfloat16 or wider, within the bound.
No kernel may reach another device: no remote copies, remote signals or barrier semaphores. Data moves between devices by JAX's collectives and lax.ppermute only.
A program may use at most 64 MiB of HBM per device.

v0:
```python
import jax
import jax.numpy as jnp
from jax import lax
from jax.sharding import PartitionSpec as P

epsilon = 1e-05


def cut_along(value, dim, size):
    lengths = value.shape
    tiles = value.reshape(*lengths[:dim], size, lengths[dim] // size, *lengths[dim + 1 :])
    return jnp.moveaxis(tiles, dim, 0)


def sum_at_owner(value, axis, dim):
    size = lax.axis_size(axis)
    tiles = lax.all_to_all(cut_along(value, dim, size), axis, 0, 0, tiled=True)
    return jnp.sum(tiles, axis=0)


def layer_norm(values, scales):
    average = jnp.mean(values, axis=-1, keepdims=True)
    centred = values - average
    variance = jnp.mean(centred * centred, axis=-1, keepdims=True)
    return centred * lax.rsqrt(variance + epsilon) * scales


def edge_change(edge_rows, sender_feat, receiver_feat, edge_w1, edge_b1, edge_w2, edge_gain):
    latent = edge_rows.shape[1]
    first = jnp.dot(edge_rows, edge_w1[:latent], preferred_element_type=jnp.float32)
    first = first + jnp.dot(
        sender_feat, edge_w1[latent : 2 * latent], preferred_element_type=jnp.float32
    )
    first = first + jnp.dot(
        receiver_feat, edge_w1[2 * latent :], preferred_element_type=jnp.float32
    )
    hidden = jax.nn.silu(first + edge_b1).astype(jnp.bfloat16)
    return layer_norm(jnp.dot(hidden, edge_w2, preferred_element_type=jnp.float32), edge_gain)


def node_change(node_rows, incoming, node_w1, node_b1, node_w2, node_gain):
    latent = node_rows.shape[1]
    first = jnp.dot(node_rows, node_w1[:latent], preferred_element_type=jnp.float32)
    first = first + jnp.dot(incoming, node_w1[latent:], preferred_element_type=jnp.float32)
    hidden = jax.nn.silu(first + node_b1).astype(jnp.bfloat16)
    return layer_norm(jnp.dot(hidden, node_w2, preferred_element_type=jnp.float32), node_gain)


def local(
    nodes,
    edges,
    receivers,
    sender_slot,
    send_rows,
    live_edges,
    edge_w1,
    edge_b1,
    edge_w2,
    edge_gain,
    node_w1,
    node_b1,
    node_w2,
    node_gain,
):
    latent = nodes.shape[1]
    edge_count = edges.shape[0]
    patch_rows = lax.all_gather(nodes, "feat", axis=0, tiled=True)
    patch_count = patch_rows.shape[0]
    outgoing = send_rows[0, 0]
    packed = jnp.take(nodes, outgoing.reshape(-1), axis=0).reshape(
        outgoing.shape[0], outgoing.shape[1], latent
    )
    remote = lax.all_to_all(packed, "patch", split_axis=0, concat_axis=0, tiled=True).reshape(
        -1, latent
    )
    lookup_rows = jnp.concatenate([patch_rows, remote], axis=0)
    sender_feat = jnp.take(lookup_rows, sender_slot, axis=0)
    receiver_feat = jnp.take(patch_rows, receivers, axis=0)
    alive_count = live_edges[0]
    alive = lax.broadcasted_iota(jnp.int32, (edge_count,), 0) < alive_count
    change = edge_change(edges, sender_feat, receiver_feat, edge_w1, edge_b1, edge_w2, edge_gain)
    edges_out = (edges.astype(jnp.float32) + jnp.where(alive[:, None], change, 0.0)).astype(
        jnp.bfloat16
    )
    owner_rows = lax.broadcasted_iota(jnp.int32, (patch_count, edge_count), 0)
    one_hot = ((receivers[None, :] == owner_rows) & alive[None, :]).astype(jnp.bfloat16)
    partial_sums = jnp.dot(one_hot, edges_out, preferred_element_type=jnp.float32)
    summed = sum_at_owner(partial_sums, "feat", 0)
    incoming = summed.astype(jnp.bfloat16)
    change = node_change(nodes, incoming, node_w1, node_b1, node_w2, node_gain)
    nodes_out = (nodes.astype(jnp.float32) + change).astype(jnp.bfloat16)
    return (edges_out, nodes_out)


def solution(mesh):
    placed = (
        P(("patch", "feat"), None),
        P(("patch", "feat"), None),
        P(("patch", "feat")),
        P(("patch", "feat")),
        P("patch", "feat", None, None),
        P(("patch", "feat")),
        P(),
        P(),
        P(),
        P(),
        P(),
        P(),
        P(),
        P(),
    )
    return jax.shard_map(
        local,
        mesh=mesh,
        in_specs=placed,
        out_specs=(P(("patch", "feat"), None), P(("patch", "feat"), None)),
        check_vma=False,
    )
```

profile of v0, /device:TPU:1, one launch (start us, length us, event | category | flops | bytes accessed | tf_op | source)
XLA Modules:
  0.0 107.9 jit_solution(567308543703744715)
XLA Ops:
  0.6 0.0 copy-start
  0.6 0.8 copy.21
  1.5 0.7 compare_and_fusion
  2.2 0.1 reshape_squeeze.6
  2.3 0.1 copy.20
  2.5 5.8 %gather_fusion = bf16[1536,512]{1,0:T(8,128)(2,1)S(1)} fusion(bf16[160,512]{1,0:T(8,128)(2,1)} %param.14, s32[2048]{0:T(1024)S(1)} %pad_clamp_fusion.2), kind=kCustom, calls=%fused_computation | custom fusion | bytes 3151872 | tf_op jit(solution)/shard_map/jit(_take)/gather | solution.py:70
  8.3 1.4 %broadcast_select_fusion = bf16[64,24,512]{2,1,0:T(8,128)(2,1)} fusion(bf16[64,24,512]{2,1,0:T(8,128)(2,1)S(1)} %bitcast.18, pred[64,24]{1,0:T(8,128)(4,1)S(1)} %copy.20), kind=kLoop, calls=%fused_computation.15 | loop fusion | flops 786432 | bytes 3147264 | tf_op jit(solution)/shard_map/jit(_take)/select_n | solution.py:70
  9.7 13.0 %all-to-all-start = ((bf16[64,24,512]{2,1,0:T(8,128)(2,1)}), bf16[64,24,512]{2,1,0:T(8,128)(2,1)S(1)}, u32[]{:S(2)}, u32[]{:S(2)}) async-start(bf16[64,24,512]{2,1,0:T(8,128)(2,1)} %broadcast_select_fusion), calls=%async_computation | async-start | bytes 3145728 | tf_op jit(solution)/shard_map/all_to_all | solution.py:73
  22.7 0.0 copy-start.7
  22.7 0.0 copy-start.1
  23.4 2.4 %copy.19 = bf16[1280,512]{0,1:T(8,128)(2,1)} copy(bf16[1280,512]{1,0:T(8,128)(2,1)} %param.15) | data formatting | bytes 2621440 | tf_op args[1]
  25.8 0.0 copy-done.7
  25.8 0.0 copy-done.1
  25.8 12.0 %all_gather.3 = bf16[640,512]{1,0:T(8,128)(2,1)S(1)} all-gather(bf16[160,512]{1,0:T(8,128)(2,1)S(1)} %copy-done.1), channel_id=1, replica_groups=mesh['patch'=64,'feat'=4] {'feat'}, dimensions={0}, use_global_device_ids=true | all-gather | bytes 819200 | tf_op jit(solution)/shard_map/all_gather | solution.py:67
  37.8 0.0 copy-start.6
  37.8 4.7 %gather_fusion.2 = bf16[1280,512]{1,0:T(8,128)(2,1)} fusion(bf16[640,512]{1,0:T(8,128)(2,1)S(1)} %all_gather.3, s32[2048]{0:T(1024)S(1)} %pad_clamp_fusion), kind=kCustom, calls=%fused_computation.2 | custom fusion | bytes 2626560 | tf_op jit(solution)/shard_map/jit(_take)/gather | solution.py:78
  42.6 0.0 copy-done.6
  42.6 3.8 %fusion.25 = f32[1280,512]{1,0:T(8,128)} fusion(bf16[1280,512]{1,0:T(8,128)(2,1)} %param.15, bf16[1536,512]{1,0:T(8,128)(2,1)} %param.20), kind=kOutput, calls=%fused_computation.32 | convolution fusion | flops 671088640 | bytes 4456448 | tf_op jit(solution)/shard_map/dot_general | solution.py:30
  46.4 16.0 %all-to-all-done = bf16[64,24,512]{2,1,0:T(8,128)(2,1)S(1)} async-done(((bf16[64,24,512]{2,1,0:T(8,128)(2,1)}), bf16[64,24,512]{2,1,0:T(8,128)(2,1)S(1)}, u32[]{:S(2)}, u32[]{:S(2)}) %all-to-all-start) | async-done | bytes 1572896 | tf_op jit(solution)/shard_map/all_to_all | solution.py:73
  62.5 1.5 %pad_maximum_fusion = bf16[2176,512]{1,0:T(8,128)(2,1)} fusion(bf16[1536,512]{1,0:T(8,128)(2,1)S(1)} %bitcast.17, bf16[640,512]{1,0:T(8,128)(2,1)S(1)} %all_gather.3), kind=kLoop, calls=%fused_computation.12 | loop fusion | flops 4456448 | bytes 4456448 | tf_op jit(solution)/shard_map/concatenate | solution.py:76
  64.0 0.0 copy-start.2
  64.0 6.9 %gather_fusion.1 = bf16[1280,512]{1,0:T(8,128)(2,1)} fusion(bf16[2176,512]{1,0:T(8,128)(2,1)} %pad_maximum_fusion, s32[2048]{0:T(1024)S(1)} %pad_clamp_fusion.1), kind=kCustom, calls=%fused_computation.1 | custom fusion | bytes 2626560 | tf_op jit(solution)/shard_map/jit(_take)/gather | solution.py:77
  70.9 0.0 copy-done.2
  70.9 0.0 copy-start.10
  70.9 3.9 %convolution_add_fusion.1 = f32[1280,512]{1,0:T(8,128)} fusion(f32[1280,512]{1,0:T(8,128)S(1)} %copy-done.2, bf16[1280,512]{1,0:T(8,128)(2,1)} %gather_fusion.1, pred[1280]{0:T(1024)(128)(4,1)S(1)} %compare_and_fusion.2, bf16[1536,512]{1,0:T(8,128)(2,1)} %param.20), kind=kOutput, calls=%fused_computation.5 | convolution fusion | flops 672399360 | bytes 7079168 | tf_op jit(solution)/shard_map/dot_general | solution.py:31
  74.7 0.0 copy-done
  74.7 0.0 copy-done.10
  74.7 4.1 %fusion.42 = (f32[1280]{0:T(1024)S(1)}, f32[1280,512]{0,1:T(8,128)S(1)}) fusion(bf16[512,512]{1,0:T(8,128)(2,1)S(1)} %copy-done, f32[1280,512]{1,0:T(8,128)} %convolution_add_fusion.1, f32[512]{0:T(512)S(1)} %copy-done.10, bf16[1280,512]{1,0:T(8,128)(2,1)} %gather_fusion.2, pred[1280]{0:T(1024)(128)(4,1)S(1)} %compare_and_fusion.1, bf16[1536,512]{1,0:T(8,128)(2,1)} %param.20), kind=kOutput, calls=%fused_computation.61 | convolution fusion | flops 1348074240 | bytes 7610624 | tf_op jit(solution)/shard_map/dot_general | solution.py:38
  78.8 0.0 copy-start.3
  78.8 0.0 copy-start.8
  78.9 0.3 multiply_reduce_fusion
  79.2 1.0 copy-done.3
  80.1 0.0 copy-done.8
  80.2 0.6 add_convert_fusion
  80.8 0.0 copy-start.4
  80.8 2.1 %fusion.2 = f32[640,512]{1,0:T(8,128)} fusion(bf16[1280,512]{0,1:T(8,128)(2,1)S(1)} %add_convert_fusion, s32[1280]{0:T(1024)S(1)} %copy-done.7, pred[1280]{0:T(1024)(128)(4,1)S(1)} %iota_compare_fusion.1), kind=kOutput, calls=%fused_computation.8 | convolution fusion | flops 840499200 | bytes 2627840 | tf_op jit(solution)/shard_map/dot_general | solution.py:87
  82.9 0.0 copy-done.4
  82.9 0.0 copy-start.5
  82.9 4.3 %all-to-all-start.1 = ((f32[4,160,512]{2,1,0:T(8,128)}), f32[4,160,512]{2,1,0:T(8,128)S(1)}, u32[]{:S(2)}, u32[]{:S(2)}) async-start(f32[4,160,512]{2,1,0:T(8,128)} %bitcast.19), calls=%async_computation.1 | async-start | bytes 2621440 | tf_op jit(solution)/shard_map/all_to_all | solution.py:17
  87.2 2.0 %fusion.20 = f32[160,512]{1,0:T(8,128)} fusion(bf16[160,512]{1,0:T(8,128)(2,1)S(1)} %copy-done.1, bf16[1024,512]{1,0:T(8,128)(2,1)} %param.24), kind=kOutput, calls=%fused_computation.28 | convolution fusion | flops 83886080 | bytes 1015808 | tf_op jit(solution)/shard_map/dot_general | solution.py:43
  89.3 0.0 copy-done.5
  89.3 0.0 copy-start.11
  89.3 1.5 %copy.22 = bf16[1280,512]{1,0:T(8,128)(2,1)} copy(bf16[1280,512]{0,1:T(8,128)(2,1)S(1)} %copy-done.5) | data formatting | bytes 2621440
  90.8 14.1 %all-to-all-done.1 = f32[4,160,512]{2,1,0:T(8,128)S(1)} async-done(((f32[4,160,512]{2,1,0:T(8,128)}), f32[4,160,512]{2,1,0:T(8,128)S(1)}, u32[]{:S(2)}, u32[]{:S(2)}) %all-to-all-start.1) | async-done | bytes 1310752 | tf_op jit(solution)/shard_map/all_to_all | solution.py:17
  104.8 0.1 reduce_sum.47
  104.9 0.0 copy-done.11
  105.0 0.0 copy-start.9
  105.0 1.9 %fusion.47 = (f32[160]{0:T(256)S(1)}, f32[160,512]{1,0:T(8,128)S(1)}) fusion(bf16[512,512]{1,0:T(8,128)(2,1)} %param.26, f32[160,512]{1,0:T(8,128)} %fusion.20, bf16[1024,512]{1,0:T(8,128)(2,1)} %param.24, f32[512]{0:T(512)S(1)} %copy-done.11, bf16[160,512]{1,0:T(8,128)(2,1)S(1)} %reduce_sum.47), kind=kOutput, calls=%fused_computation.62 | convolution fusion | flops 168427360 | bytes 1870464 | tf_op jit(solution)/shard_map/dot_general | solution.py:46
  106.9 0.2 multiply_reduce_fusion.1
  107.1 0.0 copy-done.9
  107.1 0.8 add_convert_fusion.1
  (13 shorter events, 0.1 us)
Async XLA Ops:
  0.6 74.1 %copy-start = (bf16[512,512]{1,0:T(8,128)(2,1)S(1)}, bf16[512,512]{1,0:T(8,128)(2,1)}, u32[]{:S(2)}) copy-start(bf16[512,512]{1,0:T(8,128)(2,1)} %param.22) | copy-start | bytes 1572868
  9.7 52.8 %all-to-all-start = ((bf16[64,24,512]{2,1,0:T(8,128)(2,1)}), bf16[64,24,512]{2,1,0:T(8,128)(2,1)S(1)}, u32[]{:S(2)}, u32[]{:S(2)}) async-start(bf16[64,24,512]{2,1,0:T(8,128)(2,1)} %broadcast_select_fusion), calls=%async_computation | async-start | bytes 3145728 | tf_op jit(solution)/shard_map/all_to_all | solution.py:73
  22.7 3.1 %copy-start.7 = (s32[1280]{0:T(1024)S(1)}, s32[1280]{0:T(1024)}, u32[]{:S(2)}) copy-start(s32[1280]{0:T(1024)} %param.16) | copy-start | bytes 15364
  22.7 3.1 %copy-start.1 = (bf16[160,512]{1,0:T(8,128)(2,1)S(1)}, bf16[160,512]{1,0:T(8,128)(2,1)}, u32[]{:S(2)}) copy-start(bf16[160,512]{1,0:T(8,128)(2,1)} %param.14) | copy-start | bytes 491524
  37.8 4.7 %copy-start.6 = (s32[1280]{0:T(1024)S(1)}, s32[1280]{0:T(1024)}, u32[]{:S(2)}) copy-start(s32[1280]{0:T(1024)} %param.17) | copy-start | bytes 15364
  64.0 6.9 %copy-start.2 = (f32[1280,512]{1,0:T(8,128)S(1)}, f32[1280,512]{1,0:T(8,128)}, u32[]{:S(2)}) copy-start(f32[1280,512]{1,0:T(8,128)} %fusion.25) | copy-start | bytes 7864324
  70.9 3.9 %copy-start.10 = (f32[512]{0:T(512)S(1)}, f32[512]{0:T(512)}, u32[]{:S(2)}) copy-start(f32[512]{0:T(512)} %param.21) | copy-start | bytes 6148
  78.8 1.3 %copy-start.3 = (bf16[1280,512]{0,1:T(8,128)(2,1)S(1)}, bf16[1280,512]{0,1:T(8,128)(2,1)}, u32[]{:S(2)}) copy-start(bf16[1280,512]{0,1:T(8,128)(2,1)} %copy.19) | copy-start | bytes 3932164
  78.8 1.3 %copy-start.8 = (f32[512]{0:T(512)S(1)}, f32[512]{0:T(512)}, u32[]{:S(2)}) copy-start(f32[512]{0:T(512)} %param.23) | copy-start | bytes 6148
  80.8 2.1 %copy-start.4 = (bf16[1280,512]{0,1:T(8,128)(2,1)}, bf16[1280,512]{0,1:T(8,128)(2,1)S(1)}, u32[]{:S(2)}) copy-start(bf16[1280,512]{0,1:T(8,128)(2,1)S(1)} %add_convert_fusion) | copy-start | bytes 3932164
  82.9 6.3 %copy-start.5 = (bf16[1280,512]{0,1:T(8,128)(2,1)S(1)}, bf16[1280,512]{0,1:T(8,128)(2,1)}, u32[]{:S(2)}) copy-start(bf16[1280,512]{0,1:T(8,128)(2,1)} %copy-done.4) | copy-start | bytes 3932164
  82.9 21.9 %all-to-all-start.1 = ((f32[4,160,512]{2,1,0:T(8,128)}), f32[4,160,512]{2,1,0:T(8,128)S(1)}, u32[]{:S(2)}, u32[]{:S(2)}) async-start(f32[4,160,512]{2,1,0:T(8,128)} %bitcast.19), calls=%async_computation.1 | async-start | bytes 2621440 | tf_op jit(solution)/shard_map/all_to_all | solution.py:17
  89.3 15.7 %copy-start.11 = (f32[512]{0:T(512)S(1)}, f32[512]{0:T(512)}, u32[]{:S(2)}) copy-start(f32[512]{0:T(512)} %param.25) | copy-start | bytes 6148
  105.0 2.1 %copy-start.9 = (f32[512]{0:T(512)S(1)}, f32[512]{0:T(512)}, u32[]{:S(2)}) copy-start(f32[512]{0:T(512)} %param.27) | copy-start | bytes 6148
where the time goes:
time: 108 us
  waiting for transfers between devices  30.1 us (28%)
  local copies, waits for them, and re-layouts  23.4 us (22%)
  matrix products  17.8 us (16%)
  starting transfers between devices  17.3 us (16%)
  blocking collectives  12 us (11%)
  other arithmetic  5.84 us (5%)
  between operations  1.51 us (1%)
    all_to_all x1, waiting for transfers between devices, local(): lax.all_to_all(packed, 'patch', split_axis=0, concat_axis=0, tiled=True)  16 us
    all_to_all x1, waiting for transfers between devices, sum_at_owner(): tiles = lax.all_to_all(cut_along(value, dim, size), axis, 0, 0, tiled=True)  14.1 us
    all_to_all x1, starting transfers between devices, local(): lax.all_to_all(packed, 'patch', split_axis=0, concat_axis=0, tiled=True)  13 us
    all_gather x1, blocking collectives, local(): patch_rows = lax.all_gather(nodes, 'feat', axis=0, tiled=True)  12 us
    gather x1, local copies, waits for them, and re-layouts, local(): sender_feat = jnp.take(lookup_rows, sender_slot, axis=0)  6.87 us
    gather x1, local copies, waits for them, and re-layouts, local(): jnp.take(nodes, outgoing.reshape(-1), axis=0)  5.8 us
    unnamed x27, local copies, waits for them, and re-layouts  5.78 us
    gather x1, local copies, waits for them, and re-layouts, local(): receiver_feat = jnp.take(patch_rows, receivers, axis=0)  4.72 us
  transfers between devices with their start and end apart: 2, of which 2 were waited for; matrix products, arithmetic and copies ran while one was open for 13% of the time, Pallas kernels for 0%

commit v1 on v0

--- a/solution.py
+++ b/solution.py
@@ -4,6 +4,13 @@
 from jax.sharding import PartitionSpec as P
 
 epsilon = 1e-05
+
+
+def swapped_in(block, mesh_axis, dim):
+    size = lax.axis_size(mesh_axis)
+    blocks = jnp.stack([block for _ in range(size)])
+    blocks = lax.all_to_all(blocks, mesh_axis, split_axis=0, concat_axis=0)
+    return jnp.concatenate(blocks, axis=dim)
 
 
 def cut_along(value, dim, size):
@@ -64,7 +71,7 @@
 ):
     latent = nodes.shape[1]
     edge_count = edges.shape[0]
-    patch_rows = lax.all_gather(nodes, "feat", axis=0, tiled=True)
+    patch_rows = swapped_in(nodes, "feat", 0)
     patch_count = patch_rows.shape[0]
     outgoing = send_rows[0, 0]
     packed = jnp.take(nodes, outgoing.reshape(-1), axis=0).reshape(

time: 108 us -> 116 us (1.074)
  waiting for transfers between devices: 30.1 us -> 44.8 us
  blocking collectives: 12 us -> 0 us
  starting transfers between devices: 17.3 us -> 23.1 us
    all_to_all x1, waiting for transfers between devices: 16 us -> 28.1 us  [local(): lax.all_to_all(packed, 'patch', split_axis=0, concat_axis=0, tiled=True)]
    all_gather x1 -> x0, blocking collectives: 12 us -> none  [local(): patch_rows = lax.all_gather(nodes, 'feat', axis=0, tiled=True)]
    all_to_all x0 -> x1, starting transfers between devices: none -> 5.01 us  [swapped_in(): blocks = lax.all_to_all(blocks, mesh_axis, split_axis=0, concat_axis=0)]
    all_to_all x0 -> x1, waiting for transfers between devices: none -> 2.34 us  [swapped_in(): blocks = lax.all_to_all(blocks, mesh_axis, split_axis=0, concat_axis=0)]
    another operation x0 -> x1, local copies, waits for them, and re-layouts: none -> 1.88 us  [swapped_in(): blocks = jnp.stack([block for _ in range(size)])]
    all_to_all x1, starting transfers between devices: 13 us -> 14.4 us  [local(): lax.all_to_all(packed, 'patch', split_axis=0, concat_axis=0, tiled=True)]
    unnamed x27 -> x29, local copies, waits for them, and re-layouts: 5.78 us -> 5.02 us
  transfers between devices with their start and end apart: 2 -> 3, of which waited for: 2 -> 3; matrix products, arithmetic and copies ran while one was open for 13% -> 18% of each run, Pallas kernels for 0% -> 0%
where the time goes in v1:
time: 116 us
  waiting for transfers between devices  44.8 us (39%)
  local copies, waits for them, and re-layouts  23.5 us (20%)
  starting transfers between devices  23.1 us (20%)
  matrix products  17.8 us (15%)
  other arithmetic  5.12 us (4%)
  between operations  1.54 us (1%)
    all_to_all x1, waiting for transfers between devices, local(): lax.all_to_all(packed, 'patch', split_axis=0, concat_axis=0, tiled=True)  28.1 us
    all_to_all x1, starting transfers between devices, local(): lax.all_to_all(packed, 'patch', split_axis=0, concat_axis=0, tiled=True)  14.4 us
    all_to_all x1, waiting for transfers between devices, sum_at_owner(): tiles = lax.all_to_all(cut_along(value, dim, size), axis, 0, 0, tiled=True)  14.4 us
    gather x1, local copies, waits for them, and re-layouts, local(): sender_feat = jnp.take(lookup_rows, sender_slot, axis=0)  6.85 us
    unnamed x29, local copies, waits for them, and re-layouts  5.02 us
    all_to_all x1, starting transfers between devices, swapped_in(): blocks = lax.all_to_all(blocks, mesh_axis, split_axis=0, concat_axis=0)  5.01 us
    gather x1, local copies, waits for them, and re-layouts, local(): jnp.take(nodes, outgoing.reshape(-1), axis=0)  4.81 us
    gather x1, local copies, waits for them, and re-layouts, local(): receiver_feat = jnp.take(patch_rows, receivers, axis=0)  4.71 us
  transfers between devices with their start and end apart: 3, of which 3 were waited for; matrix products, arithmetic and copies ran while one was open for 18% of the time, Pallas kernels for 0%

profile of v1, /device:TPU:1, one launch (start us, length us, event | category | flops | bytes accessed | tf_op | source)
XLA Modules:
  0.0 115.7 jit_solution(7735684478757411605)
XLA Ops:
  0.6 0.0 copy-start
  0.6 0.0 copy-start.1
  0.7 0.0 copy-start.6
  0.7 1.9 %stack.2 = bf16[4,160,512]{2,1,0:T(8,128)(2,1)} broadcast(bf16[160,512]{1,0:T(8,128)(2,1)} %param.14), dimensions={1,2} | broadcast | bytes 819200 | tf_op jit(solution)/shard_map/stack | solution.py:11
  2.5 5.0 %all-to-all-start = ((bf16[4,160,512]{2,1,0:T(8,128)(2,1)}), bf16[4,160,512]{2,1,0:T(8,128)(2,1)S(1)}, u32[]{:S(2)}, u32[]{:S(2)}) async-start(bf16[4,160,512]{2,1,0:T(8,128)(2,1)} %stack.2), calls=%async_computation | async-start | bytes 1310720 | tf_op jit(solution)/shard_map/all_to_all | solution.py:12
  7.6 0.0 copy-done.6
  7.6 0.1 copy.21
  7.6 0.1 reshape_squeeze.6
  7.8 0.0 copy-done.1
  7.8 4.8 %gather_fusion = bf16[1536,512]{1,0:T(8,128)(2,1)S(1)} fusion(bf16[160,512]{1,0:T(8,128)(2,1)S(1)} %copy-done.1, s32[2048]{0:T(1024)S(1)} %pad_clamp_fusion.2), kind=kCustom, calls=%fused_computation | custom fusion | bytes 3151872 | tf_op jit(solution)/shard_map/jit(_take)/gather | solution.py:77
  12.6 0.1 copy.20
  12.7 1.4 %broadcast_select_fusion = bf16[64,24,512]{2,1,0:T(8,128)(2,1)} fusion(bf16[64,24,512]{2,1,0:T(8,128)(2,1)S(1)} %bitcast.21, pred[64,24]{1,0:T(8,128)(4,1)S(1)} %copy.20), kind=kLoop, calls=%fused_computation.15 | loop fusion | flops 786432 | bytes 3147264 | tf_op jit(solution)/shard_map/jit(_take)/select_n | solution.py:77
  14.2 2.3 %all-to-all-done = bf16[4,160,512]{2,1,0:T(8,128)(2,1)S(1)} async-done(((bf16[4,160,512]{2,1,0:T(8,128)(2,1)}), bf16[4,160,512]{2,1,0:T(8,128)(2,1)S(1)}, u32[]{:S(2)}, u32[]{:S(2)}) %all-to-all-start) | async-done | bytes 655392 | tf_op jit(solution)/shard_map/all_to_all | solution.py:12
  16.5 14.4 %all-to-all-start.1 = ((bf16[64,24,512]{2,1,0:T(8,128)(2,1)}), bf16[64,24,512]{2,1,0:T(8,128)(2,1)S(1)}, u32[]{:S(2)}, u32[]{:S(2)}) async-start(bf16[64,24,512]{2,1,0:T(8,128)(2,1)} %broadcast_select_fusion), calls=%async_computation.1 | async-start | bytes 3145728 | tf_op jit(solution)/shard_map/all_to_all | solution.py:80
  30.9 0.0 copy-start.7
  30.9 0.0 copy-start.8
  31.6 2.4 %copy.19 = bf16[1280,512]{0,1:T(8,128)(2,1)} copy(bf16[1280,512]{1,0:T(8,128)(2,1)} %param.15) | data formatting | bytes 2621440 | tf_op args[1]
  34.0 0.0 copy-done.7
  34.0 0.0 copy-done.8
  34.1 3.8 %fusion.25 = f32[1280,512]{1,0:T(8,128)} fusion(bf16[1280,512]{1,0:T(8,128)(2,1)} %param.15, bf16[1536,512]{1,0:T(8,128)(2,1)} %param.20), kind=kOutput, calls=%fused_computation.32 | convolution fusion | flops 671088640 | bytes 4456448 | tf_op jit(solution)/shard_map/dot_general | solution.py:37
  37.9 4.7 %gather_fusion.2 = bf16[1280,512]{1,0:T(8,128)(2,1)} fusion(bf16[640,512]{1,0:T(8,128)(2,1)S(1)} %bitcast.18, s32[2048]{0:T(1024)S(1)} %pad_clamp_fusion), kind=kCustom, calls=%fused_computation.2 | custom fusion | bytes 2626560 | tf_op jit(solution)/shard_map/jit(_take)/gather | solution.py:85
  42.6 28.1 %all-to-all-done.1 = bf16[64,24,512]{2,1,0:T(8,128)(2,1)S(1)} async-done(((bf16[64,24,512]{2,1,0:T(8,128)(2,1)}), bf16[64,24,512]{2,1,0:T(8,128)(2,1)S(1)}, u32[]{:S(2)}, u32[]{:S(2)}) %all-to-all-start.1) | async-done | bytes 1572896 | tf_op jit(solution)/shard_map/all_to_all | solution.py:80
  70.7 1.5 %pad_maximum_fusion = bf16[2176,512]{1,0:T(8,128)(2,1)} fusion(bf16[1536,512]{1,0:T(8,128)(2,1)S(1)} %bitcast.20, bf16[640,512]{1,0:T(8,128)(2,1)S(1)} %bitcast.19), kind=kLoop, calls=%fused_computation.12 | loop fusion | flops 4456448 | bytes 4456448 | tf_op jit(solution)/shard_map/concatenate | solution.py:83
  72.2 0.0 copy-start.2
  72.2 6.9 %gather_fusion.1 = bf16[1280,512]{1,0:T(8,128)(2,1)} fusion(bf16[2176,512]{1,0:T(8,128)(2,1)} %pad_maximum_fusion, s32[2048]{0:T(1024)S(1)} %pad_clamp_fusion.1), kind=kCustom, calls=%fused_computation.1 | custom fusion | bytes 2626560 | tf_op jit(solution)/shard_map/jit(_take)/gather | solution.py:84
  79.0 0.0 copy-done.2
  79.0 0.0 copy-start.11
  79.0 3.9 %convolution_add_fusion.1 = f32[1280,512]{1,0:T(8,128)} fusion(f32[1280,512]{1,0:T(8,128)S(1)} %copy-done.2, bf16[1280,512]{1,0:T(8,128)(2,1)} %gather_fusion.1, pred[1280]{0:T(1024)(128)(4,1)S(1)} %compare_and_fusion.2, bf16[1536,512]{1,0:T(8,128)(2,1)} %param.20), kind=kOutput, calls=%fused_computation.5 | convolution fusion | flops 672399360 | bytes 7079168 | tf_op jit(solution)/shard_map/dot_general | solution.py:38
  82.9 0.0 copy-done
  82.9 0.0 copy-done.11
  82.9 4.1 %fusion.42 = (f32[1280]{0:T(1024)S(1)}, f32[1280,512]{0,1:T(8,128)S(1)}) fusion(bf16[512,512]{1,0:T(8,128)(2,1)S(1)} %copy-done, f32[1280,512]{1,0:T(8,128)} %convolution_add_fusion.1, f32[512]{0:T(512)S(1)} %copy-done.11, bf16[1280,512]{1,0:T(8,128)(2,1)} %gather_fusion.2, pred[1280]{0:T(1024)(128)(4,1)S(1)} %compare_and_fusion.1, bf16[1536,512]{1,0:T(8,128)(2,1)} %param.20), kind=kOutput, calls=%fused_computation.61 | convolution fusion | flops 1348074240 | bytes 7610624 | tf_op jit(solution)/shard_map/dot_general | solution.py:45
  87.0 0.0 copy-start.3
  87.0 0.0 copy-start.9
  87.0 0.3 multiply_reduce_fusion
  87.4 1.0 copy-done.3
  88.3 0.0 copy-done.9
  88.3 0.6 add_convert_fusion
  89.0 0.0 copy-start.4
  89.0 2.1 %fusion.2 = f32[640,512]{1,0:T(8,128)} fusion(bf16[1280,512]{0,1:T(8,128)(2,1)S(1)} %add_convert_fusion, s32[1280]{0:T(1024)S(1)} %copy-done.8, pred[1280]{0:T(1024)(128)(4,1)S(1)} %iota_compare_fusion.1), kind=kOutput, calls=%fused_computation.8 | convolution fusion | flops 840499200 | bytes 2627840 | tf_op jit(solution)/shard_map/dot_general | solution.py:94
  91.1 0.0 copy-done.4
  91.1 0.0 copy-start.5
  91.1 3.7 %all-to-all-start.2 = ((f32[4,160,512]{2,1,0:T(8,128)}), f32[4,160,512]{2,1,0:T(8,128)S(1)}, u32[]{:S(2)}, u32[]{:S(2)}) async-start(f32[4,160,512]{2,1,0:T(8,128)} %bitcast.22), calls=%async_computation.2 | async-start | bytes 2621440 | tf_op jit(solution)/shard_map/all_to_all | solution.py:24
  94.8 2.0 %fusion.20 = f32[160,512]{1,0:T(8,128)} fusion(bf16[160,512]{1,0:T(8,128)(2,1)S(1)} %copy-done.1, bf16[1024,512]{1,0:T(8,128)(2,1)} %param.24), kind=kOutput, calls=%fused_computation.28 | convolution fusion | flops 83886080 | bytes 1015808 | tf_op jit(solution)/shard_map/dot_general | solution.py:50
  96.8 0.0 copy-done.5
  96.8 0.0 copy-start.12
  96.8 1.5 %copy.22 = bf16[1280,512]{1,0:T(8,128)(2,1)} copy(bf16[1280,512]{0,1:T(8,128)(2,1)S(1)} %copy-done.5) | data formatting | bytes 2621440
  98.3 14.4 %all-to-all-done.2 = f32[4,160,512]{2,1,0:T(8,128)S(1)} async-done(((f32[4,160,512]{2,1,0:T(8,128)}), f32[4,160,512]{2,1,0:T(8,128)S(1)}, u32[]{:S(2)}, u32[]{:S(2)}) %all-to-all-start.2) | async-done | bytes 1310752 | tf_op jit(solution)/shard_map/all_to_all | solution.py:24
  112.6 0.1 reduce_sum.47
  112.8 0.0 copy-done.12
  112.8 0.0 copy-start.10
  112.8 1.9 %fusion.47 = (f32[160]{0:T(256)S(1)}, f32[160,512]{1,0:T(8,128)S(1)}) fusion(bf16[512,512]{1,0:T(8,128)(2,1)} %param.26, f32[160,512]{1,0:T(8,128)} %fusion.20, bf16[1024,512]{1,0:T(8,128)(2,1)} %param.24, f32[512]{0:T(512)S(1)} %copy-done.12, bf16[160,512]{1,0:T(8,128)(2,1)S(1)} %reduce_sum.47), kind=kOutput, calls=%fused_computation.62 | convolution fusion | flops 168427360 | bytes 1870464 | tf_op jit(solution)/shard_map/dot_general | solution.py:53
  114.7 0.2 multiply_reduce_fusion.1
  114.9 0.0 copy-done.10
  114.9 0.8 add_convert_fusion.1
  (14 shorter events, 0.1 us)
Async XLA Ops:
  0.6 82.3 %copy-start = (bf16[512,512]{1,0:T(8,128)(2,1)S(1)}, bf16[512,512]{1,0:T(8,128)(2,1)}, u32[]{:S(2)}) copy-start(bf16[512,512]{1,0:T(8,128)(2,1)} %param.22) | copy-start | bytes 1572868
  0.6 7.1 %copy-start.1 = (bf16[160,512]{1,0:T(8,128)(2,1)S(1)}, bf16[160,512]{1,0:T(8,128)(2,1)}, u32[]{:S(2)}) copy-start(bf16[160,512]{1,0:T(8,128)(2,1)} %param.14) | copy-start | bytes 491524
  0.7 6.9 %copy-start.6 = (s32[1,1,64,24]{2,3,1,0:T(8,128)S(1)}, s32[1,1,64,24]{2,3,1,0:T(8,128)}, u32[]{:S(2)}) copy-start(s32[1,1,64,24]{2,3,1,0:T(8,128)} %param.18) | copy-start | bytes 18436
  2.5 13.9 %all-to-all-start = ((bf16[4,160,512]{2,1,0:T(8,128)(2,1)}), bf16[4,160,512]{2,1,0:T(8,128)(2,1)S(1)}, u32[]{:S(2)}, u32[]{:S(2)}) async-start(bf16[4,160,512]{2,1,0:T(8,128)(2,1)} %stack.2), calls=%async_computation | async-start | bytes 1310720 | tf_op jit(solution)/shard_map/all_to_all | solution.py:12
  16.5 54.2 %all-to-all-start.1 = ((bf16[64,24,512]{2,1,0:T(8,128)(2,1)}), bf16[64,24,512]{2,1,0:T(8,128)(2,1)S(1)}, u32[]{:S(2)}, u32[]{:S(2)}) async-start(bf16[64,24,512]{2,1,0:T(8,128)(2,1)} %broadcast_select_fusion), calls=%async_computation.1 | async-start | bytes 3145728 | tf_op jit(solution)/shard_map/all_to_all | solution.py:80
  30.9 3.1 %copy-start.7 = (s32[1280]{0:T(1024)S(1)}, s32[1280]{0:T(1024)}, u32[]{:S(2)}) copy-start(s32[1280]{0:T(1024)} %param.17) | copy-start | bytes 15364
  30.9 3.1 %copy-start.8 = (s32[1280]{0:T(1024)S(1)}, s32[1280]{0:T(1024)}, u32[]{:S(2)}) copy-start(s32[1280]{0:T(1024)} %param.16) | copy-start | bytes 15364
  72.2 6.9 %copy-start.2 = (f32[1280,512]{1,0:T(8,128)S(1)}, f32[1280,512]{1,0:T(8,128)}, u32[]{:S(2)}) copy-start(f32[1280,512]{1,0:T(8,128)} %fusion.25) | copy-start | bytes 7864324
  79.0 3.9 %copy-start.11 = (f32[512]{0:T(512)S(1)}, f32[512]{0:T(512)}, u32[]{:S(2)}) copy-start(f32[512]{0:T(512)} %param.21) | copy-start | bytes 6148
  87.0 1.3 %copy-start.3 = (bf16[1280,512]{0,1:T(8,128)(2,1)S(1)}, bf16[1280,512]{0,1:T(8,128)(2,1)}, u32[]{:S(2)}) copy-start(bf16[1280,512]{0,1:T(8,128)(2,1)} %copy.19) | copy-start | bytes 3932164
  87.0 1.3 %copy-start.9 = (f32[512]{0:T(512)S(1)}, f32[512]{0:T(512)}, u32[]{:S(2)}) copy-start(f32[512]{0:T(512)} %param.23) | copy-start | bytes 6148
  89.0 2.1 %copy-start.4 = (bf16[1280,512]{0,1:T(8,128)(2,1)}, bf16[1280,512]{0,1:T(8,128)(2,1)S(1)}, u32[]{:S(2)}) copy-start(bf16[1280,512]{0,1:T(8,128)(2,1)S(1)} %add_convert_fusion) | copy-start | bytes 3932164
  91.1 5.7 %copy-start.5 = (bf16[1280,512]{0,1:T(8,128)(2,1)S(1)}, bf16[1280,512]{0,1:T(8,128)(2,1)}, u32[]{:S(2)}) copy-start(bf16[1280,512]{0,1:T(8,128)(2,1)} %copy-done.4) | copy-start | bytes 3932164
  91.1 21.5 %all-to-all-start.2 = ((f32[4,160,512]{2,1,0:T(8,128)}), f32[4,160,512]{2,1,0:T(8,128)S(1)}, u32[]{:S(2)}, u32[]{:S(2)}) async-start(f32[4,160,512]{2,1,0:T(8,128)} %bitcast.22), calls=%async_computation.2 | async-start | bytes 2621440 | tf_op jit(solution)/shard_map/all_to_all | solution.py:24
  96.8 16.0 %copy-start.12 = (f32[512]{0:T(512)S(1)}, f32[512]{0:T(512)}, u32[]{:S(2)}) copy-start(f32[512]{0:T(512)} %param.25) | copy-start | bytes 6148
  112.8 2.1 %copy-start.10 = (f32[512]{0:T(512)S(1)}, f32[512]{0:T(512)}, u32[]{:S(2)}) copy-start(f32[512]{0:T(512)} %param.27) | copy-start | bytes 6148
